TPU v7x, 128 devices: a whole 4x4x4 slice. The times are simulated.
128 devices in a mesh: dp: 32 (over y, z, x_hi), tensor: 4 (over x_lo, core).
Axes of the slice: x: 4 (x_hi: 2, x_lo: 2; x = x_hi * 2 + x_lo), y: 4, z: 4, core: 2. Of those that a mesh axis runs over, the one named last changes fastest.
Arguments:
- tokens: bfloat16 [16384, 2048], P(('dp', 'tensor')), may hold values from -6 to 6
- segment_ids: int32 [16384], P('dp'), may hold values from 0 to 254, as said below
- norm1_gain: float32 [2048], replicated, may hold values from 0.5 to 1.5
- norm1_shift: float32 [2048], replicated, may hold values from -3 to 3
- w_query: bfloat16 [2048, 2048], P(None, 'tensor'), may hold values from -0.125 to 0.125
- w_key: bfloat16 [2048, 2048], P(None, 'tensor'), may hold values from -0.125 to 0.125
- w_value: bfloat16 [2048, 4096], P(None, 'tensor'), may hold values from -0.125 to 0.125
- w_gate: bfloat16 [2048, 4096], P(None, 'tensor'), may hold values from -0.125 to 0.125
- w_output: bfloat16 [4096, 2048], P('tensor'), may hold values from -0.09375 to 0.09375
- norm2_gain: float32 [2048], replicated, may hold values from 0.5 to 1.5
- norm2_shift: float32 [2048], replicated, may hold values from -3 to 3
- w_up: bfloat16 [2048, 4096], P(None, 'tensor'), may hold values from -0.125 to 0.125
- w_down: bfloat16 [4096, 2048], P('tensor'), may hold values from -0.09375 to 0.09375
- cotangent: bfloat16 [16384, 2048], P(('dp', 'tensor')), may hold values from -6 to 6
Outputs:
- block_out: bfloat16 [16384, 2048], P(('dp', 'tensor'))
- tokens_grad: float32 [16384, 2048], P(('dp', 'tensor'))
- norm1_gain_grad: float32 [2048], P(('dp', 'tensor'))
- norm1_shift_grad: float32 [2048], P(('dp', 'tensor'))
- query_grad: float32 [2048, 2048], P('dp', 'tensor')
- key_grad: float32 [2048, 2048], P('dp', 'tensor')
- value_grad: float32 [2048, 4096], P('dp', 'tensor')
- gate_grad: float32 [2048, 4096], P('dp', 'tensor')
- output_grad: float32 [4096, 2048], P('tensor', 'dp')
- norm2_gain_grad: float32 [2048], P(('dp', 'tensor'))
- norm2_shift_grad: float32 [2048], P(('dp', 'tensor'))
- up_grad: float32 [2048, 4096], P('dp', 'tensor')
- down_grad: float32 [4096, 2048], P('tensor', 'dp')
Inputs may be any that keep to these rules, and one draw needn't show every extreme that they name: `segment_ids`: within each packed row of 512 positions the ids never fall; rows have disjoint ids; row r's ids start at 8 * r; three document boundaries lie in the row's first eighth of positions and three in its last eighth (they may coincide), so one document spans the middle of every row.
All inputs are finite; a program needn't handle non-finite values.
Results may differ from a plain program's by a relative error of at most 0.025.
Values may be sent and summed in bfloat16 or wider, within the bound.
No kernel may reach another device: no remote copies, remote signals or barrier semaphores. Data moves between devices by JAX's collectives and lax.ppermute only.
A program may use at most 192 MiB of HBM per device.

v0:
```python
import jax
import jax.numpy as jnp
from jax import lax
from jax.sharding import PartitionSpec as P

H = 8
DK = 256
DV = 512


def norm_rows(value, epsilon):
    centred = value - jnp.mean(value, axis=-1, keepdims=True)
    factor = lax.rsqrt(jnp.mean(centred * centred, axis=-1, keepdims=True) + epsilon)
    return (centred * factor, factor)


def norm_back(grad, normed, factor):
    return factor * (
        grad
        - jnp.mean(grad, axis=-1, keepdims=True)
        - normed * jnp.mean(grad * normed, axis=-1, keepdims=True)
    )


def rotate(value, head_count, turn):
    length = value.shape[0]
    half = DK // 2
    freqs = 10000.0 ** (-jnp.arange(half, dtype=jnp.float32) / half)
    angle = jnp.arange(length, dtype=jnp.float32)[:, None] * freqs[None, :]
    cosine = jnp.cos(angle)[:, None, :]
    sine = turn * jnp.sin(angle)[:, None, :]
    split = value.reshape(length, head_count, 2, half)
    first = split[:, :, 0]
    second = split[:, :, 1]
    joined = jnp.concatenate(
        [first * cosine - second * sine, first * sine + second * cosine], axis=-1
    )
    return joined.reshape(length, head_count * DK)


def decay_table(segment, first_head, head_count):
    length = segment.shape[0]
    position = jnp.arange(length, dtype=jnp.int32)
    distance = position[:, None] - position[None, :]
    allowed = (segment[:, None] == segment[None, :]) & (distance >= 0)
    head_ids = (first_head + jnp.arange(head_count, dtype=jnp.int32)).astype(jnp.float32)
    rate = jnp.log(1.0 - 2.0 ** (-5.0 - head_ids))
    steps_back = jnp.where(allowed, distance, jnp.zeros_like(distance)).astype(jnp.float32)
    return jnp.where(allowed[None], jnp.exp(steps_back[None] * rate[:, None, None]), 0.0)


def local(
    tokens,
    segment_ids,
    norm1_gain,
    norm1_shift,
    w_query,
    w_key,
    w_value,
    w_gate,
    w_output,
    norm2_gain,
    norm2_shift,
    w_up,
    w_down,
    cotangent,
):
    length = segment_ids.shape[0]
    head_count = H // lax.axis_size("tensor")
    first_head = lax.axis_index("tensor") * head_count
    inputs = tokens.astype(jnp.float32)
    normed1, factor1 = norm_rows(inputs, 1e-05)
    hidden1_rows = (normed1 * norm1_gain + norm1_shift).astype(jnp.bfloat16)
    hidden1 = lax.all_gather(hidden1_rows, "tensor", axis=0, tiled=True)
    query_pre = jnp.dot(hidden1, w_query, preferred_element_type=jnp.float32)
    key_pre = jnp.dot(hidden1, w_key, preferred_element_type=jnp.float32)
    value_pre = jnp.dot(hidden1, w_value, preferred_element_type=jnp.float32)
    gate_pre = jnp.dot(hidden1, w_gate, preferred_element_type=jnp.float32)
    query_matrix = (
        rotate(query_pre, head_count, 1.0).astype(jnp.bfloat16).reshape(length, head_count, DK)
    )
    key_matrix = (
        rotate(key_pre, head_count, 1.0).astype(jnp.bfloat16).reshape(length, head_count, DK)
    )
    value_matrix = value_pre.astype(jnp.bfloat16).reshape(length, head_count, DV)
    decay = decay_table(segment_ids, first_head, head_count)
    unmasked_scores = jnp.einsum(
        "vqj,fqj->qvf", query_matrix, key_matrix, preferred_element_type=jnp.float32
    )
    decayed_scores = (unmasked_scores * DK ** (-0.5) * decay).astype(jnp.bfloat16)
    mixed_values = jnp.einsum(
        "fkg,gfy->kfy", decayed_scores, value_matrix, preferred_element_type=jnp.float32
    )
    group_normed, group_factor = norm_rows(mixed_values, 1.0)
    gate_sigmoid = jax.nn.sigmoid(gate_pre)
    gate_silu = gate_pre * gate_sigmoid
    group_flat = group_normed.reshape(length, head_count * DV)
    gated = (gate_silu * group_flat).astype(jnp.bfloat16)
    retention_part = lax.psum_scatter(
        jnp.dot(gated, w_output, preferred_element_type=jnp.float32),
        "tensor",
        scatter_dimension=0,
        tiled=True,
    )
    mid_rows = inputs + retention_part
    normed2, factor2 = norm_rows(mid_rows, 1e-05)
    hidden2_rows = (normed2 * norm2_gain + norm2_shift).astype(jnp.bfloat16)
    hidden2 = lax.all_gather(hidden2_rows, "tensor", axis=0, tiled=True)
    up_pre = jnp.dot(hidden2, w_up, preferred_element_type=jnp.float32)
    activated = jax.nn.gelu(up_pre, approximate=True).astype(jnp.bfloat16)
    block_out = (
        mid_rows
        + lax.psum_scatter(
            jnp.dot(activated, w_down, preferred_element_type=jnp.float32).astype(jnp.bfloat16),
            "tensor",
            scatter_dimension=0,
            tiled=True,
        ).astype(jnp.float32)
    ).astype(jnp.bfloat16)
    cot_full = lax.all_gather(cotangent, "tensor", axis=0, tiled=True)
    d_act = jnp.dot(cot_full, w_down.T, preferred_element_type=jnp.float32)
    tangent = jnp.tanh(0.7978845608 * (up_pre + 0.044715 * up_pre * up_pre * up_pre))
    slope = 0.5 * (1.0 + tangent) + 0.5 * up_pre * (1.0 - tangent * tangent) * 0.7978845608 * (
        1.0 + 3.0 * 0.044715 * up_pre * up_pre
    )
    d_up = (d_act * slope).astype(jnp.bfloat16)
    down_grad = jnp.dot(activated.T, cot_full, preferred_element_type=jnp.float32)
    up_grad = jnp.dot(hidden2.T, d_up, preferred_element_type=jnp.float32)
    d_hidden2 = lax.psum_scatter(
        jnp.dot(d_up, w_up.T, preferred_element_type=jnp.float32),
        "tensor",
        scatter_dimension=0,
        tiled=True,
    )
    gain2_part = jnp.sum(d_hidden2 * normed2, axis=0)
    shift2_part = jnp.sum(d_hidden2, axis=0)
    d_mid = cotangent.astype(jnp.float32) + norm_back(d_hidden2 * norm2_gain, normed2, factor2)
    d_mid_low = d_mid.astype(jnp.bfloat16)
    d_mid_full = lax.all_gather(d_mid_low, "tensor", axis=0, tiled=True)
    output_grad = jnp.dot(gated.T, d_mid_full, preferred_element_type=jnp.float32)
    d_gated = jnp.dot(d_mid_full, w_output.T, preferred_element_type=jnp.float32)
    d_gate_pre = (
        d_gated * group_flat * (gate_sigmoid + gate_pre * gate_sigmoid * (1.0 - gate_sigmoid))
    ).astype(jnp.bfloat16)
    d_group = (d_gated * gate_silu).reshape(length, head_count, DV)
    mixed_cotangent = norm_back(d_group, group_normed, group_factor).astype(jnp.bfloat16)
    score_cotangent = jnp.einsum(
        "vqj,fqj->qvf", mixed_cotangent, value_matrix, preferred_element_type=jnp.float32
    )
    d_value = (
        jnp.einsum(
            "jxa,xjr->ajr", decayed_scores, mixed_cotangent, preferred_element_type=jnp.float32
        )
        .reshape(length, head_count * DV)
        .astype(jnp.bfloat16)
    )
    raw_score_cotangent = (score_cotangent * DK ** (-0.5) * decay).astype(jnp.bfloat16)
    query_cotangent = jnp.einsum(
        "fkg,gfy->kfy", raw_score_cotangent, key_matrix, preferred_element_type=jnp.float32
    )
    key_cotangent = jnp.einsum(
        "jxa,xjr->ajr", raw_score_cotangent, query_matrix, preferred_element_type=jnp.float32
    )
    d_query_pre = rotate(query_cotangent.reshape(length, head_count * DK), head_count, -1.0).astype(
        jnp.bfloat16
    )
    d_key_pre = rotate(key_cotangent.reshape(length, head_count * DK), head_count, -1.0).astype(
        jnp.bfloat16
    )
    query_grad = jnp.dot(hidden1.T, d_query_pre, preferred_element_type=jnp.float32)
    key_grad = jnp.dot(hidden1.T, d_key_pre, preferred_element_type=jnp.float32)
    value_grad = jnp.dot(hidden1.T, d_value, preferred_element_type=jnp.float32)
    gate_grad = jnp.dot(hidden1.T, d_gate_pre, preferred_element_type=jnp.float32)
    total = jnp.dot(d_query_pre, w_query.T, preferred_element_type=jnp.float32)
    total = total + jnp.dot(d_key_pre, w_key.T, preferred_element_type=jnp.float32)
    total = total + jnp.dot(d_value, w_value.T, preferred_element_type=jnp.float32)
    d_hidden1 = lax.psum_scatter(
        (total + jnp.dot(d_gate_pre, w_gate.T, preferred_element_type=jnp.float32)).astype(
            jnp.bfloat16
        ),
        "tensor",
        scatter_dimension=0,
        tiled=True,
    ).astype(jnp.float32)
    gain1_part = jnp.sum(d_hidden1 * normed1, axis=0)
    shift1_part = jnp.sum(d_hidden1, axis=0)
    tokens_grad = d_mid + norm_back(d_hidden1 * norm1_gain, normed1, factor1)
    query_sum, key_sum, value_sum, gate_sum, output_sum, up_sum, down_sum = (
        lax.psum_scatter(
            query_grad.astype(jnp.bfloat16), "dp", scatter_dimension=0, tiled=True
        ).astype(jnp.float32),
        lax.psum_scatter(
            key_grad.astype(jnp.bfloat16), "dp", scatter_dimension=0, tiled=True
        ).astype(jnp.float32),
        lax.psum_scatter(
            value_grad.astype(jnp.bfloat16), "dp", scatter_dimension=0, tiled=True
        ).astype(jnp.float32),
        lax.psum_scatter(
            gate_grad.astype(jnp.bfloat16), "dp", scatter_dimension=0, tiled=True
        ).astype(jnp.float32),
        lax.psum_scatter(
            output_grad.astype(jnp.bfloat16), "dp", scatter_dimension=1, tiled=True
        ).astype(jnp.float32),
        lax.psum_scatter(
            up_grad.astype(jnp.bfloat16), "dp", scatter_dimension=0, tiled=True
        ).astype(jnp.float32),
        lax.psum_scatter(
            down_grad.astype(jnp.bfloat16), "dp", scatter_dimension=1, tiled=True
        ).astype(jnp.float32),
    )
    stacked = jnp.stack([gain1_part, shift1_part, gain2_part, shift2_part], axis=0)
    norm_sums = lax.psum_scatter(stacked, ("dp", "tensor"), scatter_dimension=1, tiled=True)
    return (
        block_out,
        tokens_grad,
        norm_sums[0],
        norm_sums[1],
        query_sum,
        key_sum,
        value_sum,
        gate_sum,
        output_sum,
        norm_sums[2],
        norm_sums[3],
        up_sum,
        down_sum,
    )


def solution(mesh):
    in_specs = (
        P(("dp", "tensor"), None),
        P("dp"),
        P(),
        P(),
        P(None, "tensor"),
        P(None, "tensor"),
        P(None, "tensor"),
        P(None, "tensor"),
        P("tensor", None),
        P(),
        P(),
        P(None, "tensor"),
        P("tensor", None),
        P(("dp", "tensor"), None),
    )
    out_specs = (
        P(("dp", "tensor"), None),
        P(("dp", "tensor"), None),
        P(("dp", "tensor")),
        P(("dp", "tensor")),
        P("dp", "tensor"),
        P("dp", "tensor"),
        P("dp", "tensor"),
        P("dp", "tensor"),
        P("tensor", "dp"),
        P(("dp", "tensor")),
        P(("dp", "tensor")),
        P("dp", "tensor"),
        P("tensor", "dp"),
    )
    return jax.shard_map(local, mesh=mesh, in_specs=in_specs, out_specs=out_specs, check_vma=False)
```

profile of v0, /device:TPU:0, one launch (start us, length us, event | category | flops | bytes accessed | tf_op | source)
XLA Modules:
  0.0 2397.0 jit_solution(15441505698840011917)
XLA Ops:
  9.9 2.3 fusion.25
  13.2 1.7 broadcast_multiply_fusion
  16.1 27.6 %all-gather.5.cloned.1.call-done = bf16[512,2048]{1,0:T(8,128)(2,1)} async-done(((bf16[128,2048]{1,0:T(8,128)(2,1)}), bf16[512,2048]{1,0:T(8,128)(2,1)}) %all-gather.5.cloned.1.call-update) | async-done | bytes 2097168 | tf_op jit(solution)/shard_map/all_gather | solution.py:74
  43.7 3.5 fusion.73
  49.6 2.9 fusion.72
  53.6 2.0 copy.104
  55.6 2.0 copy.105
  57.6 1.7 fusion.52
  60.3 1.8 copy-done.32
  62.1 2.4 convolution_convert_fusion.9
  65.8 1.7 fusion.15
  67.5 3.1 copy.101
  70.6 7.4 multiply_convert_fusion.3
  79.0 4.3 fusion.74
  83.4 46.4 %reduce-scatter.15.cloned.1.call-done = f32[128,2048]{1,0:T(8,128)} async-done(((f32[512,2048]{1,0:T(8,128)}), f32[128,2048]{1,0:T(8,128)}) %reduce-scatter.15.cloned.1.call-update) | async-done | bytes 1048592 | tf_op jit(solution)/shard_map/reduce_scatter | solution.py:99
  129.8 1.5 fusion.66
  133.4 29.4 %all-gather.7.cloned.1.call-done = bf16[512,2048]{1,0:T(8,128)(2,1)} async-done(((bf16[128,2048]{1,0:T(8,128)(2,1)}), bf16[512,2048]{1,0:T(8,128)(2,1)}) %all-gather.7.cloned.1.call-update) | async-done | bytes 2097168 | tf_op jit(solution)/shard_map/all_gather | solution.py:108
  162.8 6.5 fusion.75
  169.3 25.1 %all-gather.9.cloned.1.call-done = bf16[512,2048]{1,0:T(8,128)(2,1)} async-done(((bf16[128,2048]{1,0:T(8,128)(2,1)}), bf16[512,2048]{1,0:T(8,128)(2,1)}) %all-gather.9.cloned.1.call-update) | async-done | bytes 2097168 | tf_op jit(solution)/shard_map/all_gather | solution.py:120
  194.4 6.9 fusion.14
  202.3 4.3 fusion.76
  207.1 6.7 convolution_convert_fusion.5
  213.9 39.3 %reduce-scatter.19.cloned.1.call-done = f32[128,2048]{1,0:T(8,128)} async-done(((f32[512,2048]{1,0:T(8,128)}), f32[128,2048]{1,0:T(8,128)}) %reduce-scatter.19.cloned.1.call-update) | async-done | bytes 1048592 | tf_op jit(solution)/shard_map/reduce_scatter | solution.py:129
  253.2 1.7 multiply_reduce_fusion.2
  254.9 29.8 %reduce-scatter.17.cloned.1.call-done = bf16[128,2048]{1,0:T(8,128)(2,1)} async-done(((bf16[512,2048]{1,0:T(8,128)(2,1)}), bf16[128,2048]{1,0:T(8,128)(2,1)}) %reduce-scatter.17.cloned.1.call-update) | async-done | bytes 524304 | tf_op jit(solution)/shard_map/reduce_scatter | solution.py:113
  284.6 3.5 fusion.65
  288.2 30.0 %all-gather.11.cloned.1.call-done = bf16[512,2048]{1,0:T(8,128)(2,1)} async-done(((bf16[128,2048]{1,0:T(8,128)(2,1)}), bf16[512,2048]{1,0:T(8,128)(2,1)}) %all-gather.11.cloned.1.call-update) | async-done | bytes 2097168 | tf_op jit(solution)/shard_map/all_gather | solution.py:139
  318.2 8.7 fusion.62
  326.9 4.0 reshape.259
  330.9 4.3 copy.86
  335.1 2.3 reduce_sum.152
  337.5 2.9 multiply_reduce_fusion
  343.8 1.7 convolution_convert_fusion.8
  348.1 2.0 copy.110
  352.6 2.0 copy.109
  354.6 2.1 copy.111
  356.7 2.3 fusion.40
  360.0 1.8 pad_maximum_fusion.2
  365.6 2.4 fusion.79
  368.1 2.4 fusion.78
  370.5 3.0 add_convert_fusion
  373.6 6.7 convolution_convert_fusion
  380.3 6.2 convolution_convert_fusion.1
  386.6 4.3 convolution_convert_fusion.7
  391.0 4.3 convolution_convert_fusion.6
  395.4 7.5 reduce-scatter.21.cloned.1.call-done
  402.9 1.5 fusion.31
  406.0 6.3 convolution_convert_fusion.2
  412.6 6.2 convolution_convert_fusion.4
  418.9 6.2 convolution_convert_fusion.3
  425.1 179.2 %reduce-scatter.35.cloned.1.call-done = bf16[1024,64]{0,1:T(8,128)(2,1)} async-done(((bf16[1024,2048]{0,1:T(8,128)(2,1)}), bf16[1024,64]{0,1:T(8,128)(2,1)}) %reduce-scatter.35.cloned.1.call-update) | async-done | bytes 131088 | tf_op jit(solution)/shard_map/reduce_scatter | solution.py:207
  604.2 1.6 convert_element_type.169
  605.9 193.5 %reduce-scatter.33.cloned.1.call-done = bf16[64,1024]{1,0:T(8,128)(2,1)} async-done(((bf16[2048,1024]{1,0:T(8,128)(2,1)}), bf16[64,1024]{1,0:T(8,128)(2,1)}) %reduce-scatter.33.cloned.1.call-update) | async-done | bytes 131088 | tf_op jit(solution)/shard_map/reduce_scatter | solution.py:204
  799.4 1.6 convert_element_type.167
  801.0 183.6 %reduce-scatter.23.cloned.1.call-done = bf16[64,512]{1,0:T(8,128)(2,1)} async-done(((bf16[2048,512]{1,0:T(8,128)(2,1)}), bf16[64,512]{1,0:T(8,128)(2,1)}) %reduce-scatter.23.cloned.1.call-update) | async-done | bytes 65552 | tf_op jit(solution)/shard_map/reduce_scatter | solution.py:189
  986.1 184.5 %reduce-scatter.25.cloned.1.call-done = bf16[64,512]{1,0:T(8,128)(2,1)} async-done(((bf16[2048,512]{1,0:T(8,128)(2,1)}), bf16[64,512]{1,0:T(8,128)(2,1)}) %reduce-scatter.25.cloned.1.call-update) | async-done | bytes 65552 | tf_op jit(solution)/shard_map/reduce_scatter | solution.py:192
  1172.1 2.7 fusion.28
  1174.8 630.1 %reduce-scatter.37.cloned.1.call-done = f32[16,4]{1,0:T(8,128)} async-done(((f32[2048,4]{1,0:T(8,128)}), f32[16,4]{1,0:T(8,128)}) %reduce-scatter.37.cloned.1.call-update) | async-done | bytes 272
  1808.1 190.5 %reduce-scatter.31.cloned.1.call-done = bf16[1024,64]{0,1:T(8,128)(2,1)} async-done(((bf16[1024,2048]{0,1:T(8,128)(2,1)}), bf16[1024,64]{0,1:T(8,128)(2,1)}) %reduce-scatter.31.cloned.1.call-update) | async-done | bytes 131088 | tf_op jit(solution)/shard_map/reduce_scatter | solution.py:201
  1998.6 1.6 convert_element_type.165
  2000.2 193.3 %reduce-scatter.27.cloned.1.call-done = bf16[64,1024]{1,0:T(8,128)(2,1)} async-done(((bf16[2048,1024]{1,0:T(8,128)(2,1)}), bf16[64,1024]{1,0:T(8,128)(2,1)}) %reduce-scatter.27.cloned.1.call-update) | async-done | bytes 131088 | tf_op jit(solution)/shard_map/reduce_scatter | solution.py:195
  2193.6 1.6 convert_element_type.161
  2195.2 193.2 %reduce-scatter.29.cloned.1.call-done = bf16[64,1024]{1,0:T(8,128)(2,1)} async-done(((bf16[2048,1024]{1,0:T(8,128)(2,1)}), bf16[64,1024]{1,0:T(8,128)(2,1)}) %reduce-scatter.29.cloned.1.call-update) | async-done | bytes 131088 | tf_op jit(solution)/shard_map/reduce_scatter | solution.py:198
  2388.4 1.6 convert_element_type.163
  (156 shorter events, 36.7 us)
Async XLA Ops:
  7.2 42.4 %copy-start = (bf16[2048,512]{1,0:T(8,128)(2,1)S(1)}, bf16[2048,512]{1,0:T(8,128)(2,1)}, u32[]{:S(2)}) copy-start(bf16[2048,512]{1,0:T(8,128)(2,1)} %param.18) | copy-start | bytes 6291460
  7.2 5.1 copy-start.27
  7.2 36.5 %all-gather.5.cloned.1.call-start = ((), (), s32[]{:S(2)}) async-start(), calls=%async_computation.12 | async-start | bytes 2621440 | tf_op jit(solution)/shard_map/all_gather | solution.py:74
  12.2 117.6 %reduce-scatter.15.cloned.1.call-start = ((), (), s32[]{:S(2)}) async-start(), calls=%async_computation.13 | async-start | bytes 5242880 | tf_op jit(solution)/shard_map/reduce_scatter | solution.py:99
  57.6 1.7 copy-start.21
  57.6 1.8 copy-start.23
  57.6 2.7 copy-start.34
  59.3 0.9 copy-start.8
  59.4 0.9 copy-start.10
  59.4 0.9 copy-start.12
  59.4 0.9 copy-start.14
  59.4 2.7 copy-start.32
  62.1 2.4 copy-start.17
  64.4 1.0 copy-start.19
  65.5 2.0 copy-start.1
  70.6 8.4 copy-start.30
  78.0 1.0 copy-start.38
  83.3 48.3 %copy-start.25 = (f32[2048]{0:T(1024)S(1)}, f32[2048]{0:T(1024)}, u32[]{:S(2)}) copy-start(f32[2048]{0:T(1024)} %param.23) | copy-start | bytes 24580
  83.3 48.3 %copy-start.28 = (f32[2048]{0:T(1024)S(1)}, f32[2048]{0:T(1024)}, u32[]{:S(2)}) copy-start(f32[2048]{0:T(1024)} %param.24) | copy-start | bytes 24580
  83.3 79.5 %all-gather.7.cloned.1.call-start = ((), (), s32[]{:S(2)}) async-start(), calls=%async_computation.14 | async-start | bytes 2621440 | tf_op jit(solution)/shard_map/all_gather | solution.py:108
  132.7 61.7 %all-gather.9.cloned.1.call-start = ((), (), s32[]{:S(2)}) async-start(), calls=%async_computation.16 | async-start | bytes 2621440 | tf_op jit(solution)/shard_map/all_gather | solution.py:120
  133.3 119.9 %reduce-scatter.19.cloned.1.call-start = ((), (), s32[]{:S(2)}) async-start(), calls=%async_computation.17 | async-start | bytes 5242880 | tf_op jit(solution)/shard_map/reduce_scatter | solution.py:129
  194.4 7.9 copy-start.29
  201.3 1.0 copy-start.37
  206.7 78.0 %reduce-scatter.17.cloned.1.call-start = ((), (), s32[]{:S(2)}) async-start(), calls=%async_computation.15 | async-start | bytes 2621440 | tf_op jit(solution)/shard_map/reduce_scatter | solution.py:113
  213.8 104.3 %all-gather.11.cloned.1.call-start = ((), (), s32[]{:S(2)}) async-start(), calls=%async_computation.18 | async-start | bytes 2621440 | tf_op jit(solution)/shard_map/all_gather | solution.py:139
  288.1 114.8 %reduce-scatter.21.cloned.1.call-start = ((), (), s32[]{:S(2)}) async-start(), calls=%async_computation.19 | async-start | bytes 2621440 | tf_op jit(solution)/shard_map/reduce_scatter | solution.py:177
  337.5 3.0 copy-start.2
  337.5 3.5 copy-start.3
  341.0 1.2 copy-start.20
  341.0 1.5 copy-start.22
  341.0 1.6 copy-start.24
  342.6 1.2 copy-start.18
  343.8 1.7 copy-start.13
  343.8 1.7 copy-start.15
  345.5 1.0 copy-start.9
  345.5 1.0 copy-start.11
  351.3 5.4 copy-start.6
  359.1 0.9 copy-start.16
  363.1 2.2 copy-start.31
  363.1 2.5 copy-start.36
  365.6 2.4 copy-start.33
  365.6 2.5 copy-start.35
  368.0 2.4 copy-start.5
  373.5 230.7 %reduce-scatter.35.cloned.1.call-start = ((), (), s32[]{:S(2)}) async-start(), calls=%async_computation.26 | async-start | bytes 4325376 | tf_op jit(solution)/shard_map/reduce_scatter | solution.py:207
  380.3 419.1 %reduce-scatter.33.cloned.1.call-start = ((), (), s32[]{:S(2)}) async-start(), calls=%async_computation.25 | async-start | bytes 4325376 | tf_op jit(solution)/shard_map/reduce_scatter | solution.py:204
  386.6 598.0 %reduce-scatter.23.cloned.1.call-start = ((), (), s32[]{:S(2)}) async-start(), calls=%async_computation.20 | async-start | bytes 2162688 | tf_op jit(solution)/shard_map/reduce_scatter | solution.py:189
  391.0 779.7 %reduce-scatter.25.cloned.1.call-start = ((), (), s32[]{:S(2)}) async-start(), calls=%async_computation.21 | async-start | bytes 2162688 | tf_op jit(solution)/shard_map/reduce_scatter | solution.py:192
  395.3 7.6 copy-start.4
  395.3 7.6 copy-start.26
  395.4 1409.5 %reduce-scatter.37.cloned.1.call-start = ((), (), s32[]{:S(2)}) async-start(), calls=%async_computation.27 | async-start | bytes 1056768
  406.0 1592.7 %reduce-scatter.31.cloned.1.call-start = ((), (), s32[]{:S(2)}) async-start(), calls=%async_computation.24 | async-start | bytes 4325376 | tf_op jit(solution)/shard_map/reduce_scatter | solution.py:201
  412.3 1781.3 %reduce-scatter.27.cloned.1.call-start = ((), (), s32[]{:S(2)}) async-start(), calls=%async_computation.22 | async-start | bytes 4325376 | tf_op jit(solution)/shard_map/reduce_scatter | solution.py:195
  418.8 1969.6 %reduce-scatter.29.cloned.1.call-start = ((), (), s32[]{:S(2)}) async-start(), calls=%async_computation.23 | async-start | bytes 4325376 | tf_op jit(solution)/shard_map/reduce_scatter | solution.py:198
  425.1 747.1 %copy-start.7 = (bf16[128,2048]{1,0:T(8,128)(2,1)S(1)}, bf16[128,2048]{1,0:T(8,128)(2,1)}, u32[]{:S(2)}) copy-start(bf16[128,2048]{1,0:T(8,128)(2,1)} %reduce-scatter.21.cloned.1.call-done) | copy-start | bytes 1572868
Sparse Core Ops, SparseCore 0:
  12.3 31.3 all-gather.4
  83.4 46.3 reduce-scatter.14
  132.9 29.8 all-gather.6
  164.4 29.9 all-gather.8
  206.8 46.3 reduce-scatter.18
  255.5 29.1 reduce-scatter.16
  288.3 29.8 all-gather.10
  373.6 29.2 reduce-scatter.20
  405.3 198.8 reduce-scatter.34
  606.5 192.8 reduce-scatter.32
  801.8 182.7 reduce-scatter.22
  986.9 183.6 reduce-scatter.24
  1173.0 631.8 reduce-scatter.36
  1807.2 191.3 reduce-scatter.30
  2001.0 192.5 reduce-scatter.26
  2195.9 192.4 reduce-scatter.28
where the time goes:
time: 2410 us; the launch traced here: 2400 us
  waiting for transfers between devices  2180 us (90%)
  matrix products  108 us (4%)
  other arithmetic  45.8 us (2%)
  local copies, waits for them, and re-layouts  42.7 us (2%)
    unnamed x17, waiting for transfers between devices  631 us
    reduce_scatter x1, waiting for transfers between devices, local(): lax.psum_scatter(up_grad.astype(jnp.bfloat16), 'dp', scatter_dimension=0,...  194 us
    reduce_scatter x1, waiting for transfers between devices, local(): lax.psum_scatter(value_grad.astype(jnp.bfloat16), 'dp', scatter_dimension...  193 us
    reduce_scatter x1, waiting for transfers between devices, local(): lax.psum_scatter(gate_grad.astype(jnp.bfloat16), 'dp', scatter_dimension=...  193 us
    reduce_scatter x1, waiting for transfers between devices, local(): lax.psum_scatter(output_grad.astype(jnp.bfloat16), 'dp', scatter_dimensio...  190 us
    reduce_scatter x1, waiting for transfers between devices, local(): lax.psum_scatter(key_grad.astype(jnp.bfloat16), 'dp', scatter_dimension=0...  185 us
    reduce_scatter x1, waiting for transfers between devices, local(): lax.psum_scatter(query_grad.astype(jnp.bfloat16), 'dp', scatter_dimension...  184 us
    reduce_scatter x1, waiting for transfers between devices, local(): lax.psum_scatter(down_grad.astype(jnp.bfloat16), 'dp', scatter_dimension=...  179 us
  transfers between devices with their start and end apart: 16, of which 16 were waited for; matrix products, arithmetic and copies ran while one was open for 3% of the time, Pallas kernels for 0%

commit v1 on v0

v1 whole, which is shorter than its diff:
```python
import jax
import jax.numpy as jnp
from jax import lax
from jax.sharding import PartitionSpec as P

H = 8
DK = 256
DV = 512
F32 = jnp.float32
BF = jnp.bfloat16
SHIFTS = (1, -1, 2)


def shift_y(value, step):
    return lax.ppermute(
        value, "dp", [(i, ((i // 8 + step) % 4) * 8 + i % 8) for i in range(32)]
    )


def shift_z(value, step):
    return lax.ppermute(
        value,
        "dp",
        [(i, (i // 8) * 8 + ((i // 2 % 4 + step) % 4) * 2 + i % 2) for i in range(32)],
    )


def swap_xh(value):
    return lax.ppermute(value, "dp", [(i, i ^ 1) for i in range(32)])


def swap_xl(value):
    return lax.ppermute(value, "tensor", [(i, i ^ 2) for i in range(4)])


def swap_core(value):
    return lax.ppermute(value, "tensor", [(i, i ^ 1) for i in range(4)])


def gather_row(own):
    across = swap_xl(own)
    return jnp.concatenate([own, across, swap_core(own), swap_core(across)], axis=0)


def scatter_row(parts, wide):
    quarter = parts.shape[0] // 4
    far = parts[quarter : 2 * quarter] + swap_core(parts[3 * quarter :].astype(wide)).astype(F32)
    near = parts[:quarter] + swap_core(parts[2 * quarter : 3 * quarter].astype(wide)).astype(F32)
    return near + swap_xl(far.astype(BF)).astype(F32)


def dot(left, right):
    return jnp.dot(left, right, preferred_element_type=F32)


def dot_tn(left, right):
    return lax.dot_general(left, right, (((0,), (0,)), ((), ())), preferred_element_type=F32)


def dot_nt(left, right):
    return lax.dot_general(left, right, (((1,), (1,)), ((), ())), preferred_element_type=F32)


def norm_rows(value, epsilon):
    centred = value - jnp.mean(value, axis=-1, keepdims=True)
    factor = lax.rsqrt(jnp.mean(centred * centred, axis=-1, keepdims=True) + epsilon)
    return (centred * factor, factor)


def norm_back(grad, normed, factor):
    return factor * (
        grad
        - jnp.mean(grad, axis=-1, keepdims=True)
        - normed * jnp.mean(grad * normed, axis=-1, keepdims=True)
    )


def rotate(value, cosine, sine):
    half = DK // 2
    first = value[:, :half]
    second = value[:, half:]
    return jnp.concatenate(
        [first * cosine - second * sine, first * sine + second * cosine], axis=-1
    )


def piece(value, index, size, axis):
    return lax.dynamic_slice_in_dim(value, index * size, size, axis)


def model_slice(value, index, along):
    if along == "y":
        return piece(value, index, 512, 1)
    rows = value.shape[0]
    split = value.reshape(rows, 4, 4, 128)
    return lax.dynamic_index_in_dim(split, index, 2, keepdims=False).reshape(rows, 512)


def spread_left(left, along, place, shift):
    half = left.shape[0] // 2
    got = []
    for step in SHIFTS:
        mine = shift(model_slice(left[:half], (place + step) % 4, along), step)
        got.append(jnp.concatenate([mine, swap_core(mine)], axis=0))
    return [model_slice(left, place, along)] + got


def finish(total, place, shift, half_x):
    low = total.astype(BF)
    mine = piece(total, place, 128, 0)
    for step in SHIFTS:
        mine = mine + shift(piece(low, (place + step) % 4, 128, 0), step).astype(F32)
    other = piece(mine, 1 - half_x, 64, 0).astype(BF)
    return piece(mine, half_x, 64, 0) + swap_xh(other).astype(F32)


def local(
    tokens,
    segment_ids,
    norm1_gain,
    norm1_shift,
    w_query,
    w_key,
    w_value,
    w_gate,
    w_output,
    norm2_gain,
    norm2_shift,
    w_up,
    w_down,
    cotangent,
):
    tensor = lax.axis_index("tensor")
    dp = lax.axis_index("dp")
    y, z, xh = dp // 8, dp // 2 % 4, dp % 2
    inputs = tokens.astype(F32)
    normed1, factor1 = norm_rows(inputs, 1e-05)
    hidden1_rows = (normed1 * norm1_gain + norm1_shift).astype(BF)
    hidden1 = gather_row(hidden1_rows)
    cot_full = gather_row(cotangent)

    blocks = [tensor, tensor ^ 2, tensor ^ 1, tensor ^ 3]
    position = jnp.concatenate([b * 128 + jnp.arange(128, dtype=jnp.int32) for b in blocks])
    segment = jnp.concatenate([piece(segment_ids, b, 128, 0) for b in blocks])
    half = DK // 2
    freqs = 10000.0 ** (-jnp.arange(half, dtype=F32) / half)
    angle = position.astype(F32)[:, None] * freqs[None, :]
    cosine, sine = jnp.cos(angle), jnp.sin(angle)
    distance = position[:, None] - position[None, :]
    allowed = (segment[:, None] == segment[None, :]) & (distance >= 0)
    steps_back = jnp.where(allowed, distance, 0).astype(F32)

    hidden1_all = [hidden1]
    for step in SHIFTS:
        mine = shift_y(hidden1[:256], step)
        hidden1_all.append(jnp.concatenate([mine, swap_core(mine)], axis=0))

    query_pre = dot(hidden1, w_query)
    key_pre = dot(hidden1, w_key)
    value_low = dot(hidden1, w_value).astype(BF)
    gate_pre = dot(hidden1, w_gate)
    heads = []
    gated_parts = []
    for h in range(2):
        rate = jnp.log(1.0 - 2.0 ** (-5.0 - (tensor * 2 + h).astype(F32)))
        decay = jnp.where(allowed, jnp.exp(steps_back * rate), 0.0) * DK ** (-0.5)
        keys = slice(h * DK, (h + 1) * DK)
        vals = slice(h * DV, (h + 1) * DV)
        query = rotate(query_pre[:, keys], cosine, sine).astype(BF)
        key = rotate(key_pre[:, keys], cosine, sine).astype(BF)
        value = value_low[:, vals]
        scores = (dot_nt(query, key) * decay).astype(BF)
        mixed = dot(scores, value)
        group, group_factor = norm_rows(mixed, 1.0)
        gate = gate_pre[:, vals]
        sigmoid = jax.nn.sigmoid(gate)
        silu = gate * sigmoid
        gated_parts.append((silu * group).astype(BF))
        heads.append((decay, query, key, value, scores, group, group_factor, gate, sigmoid, silu))
    gated = jnp.concatenate(gated_parts, axis=1)

    mid_rows = inputs + scatter_row(dot(gated, w_output), BF)
    normed2, factor2 = norm_rows(mid_rows, 1e-05)
    hidden2_rows = (normed2 * norm2_gain + norm2_shift).astype(BF)
    hidden2 = gather_row(hidden2_rows)

    d_act = dot_nt(cot_full, w_down)
    up_pre = dot(hidden2, w_up)
    tangent = jnp.tanh(0.7978845608 * (up_pre + 0.044715 * up_pre * up_pre * up_pre))
    activated = (0.5 * up_pre * (1.0 + tangent)).astype(BF)
    slope = 0.5 * (1.0 + tangent) + 0.5 * up_pre * (1.0 - tangent * tangent) * 0.7978845608 * (
        1.0 + 3.0 * 0.044715 * up_pre * up_pre
    )
    d_up = (d_act * slope).astype(BF)
    d_hidden2 = scatter_row(dot_nt(d_up, w_up), BF)
    gain2_part = jnp.sum(d_hidden2 * normed2, axis=0)
    shift2_part = jnp.sum(d_hidden2, axis=0)
    d_mid = cotangent.astype(F32) + norm_back(d_hidden2 * norm2_gain, normed2, factor2)
    d_mid_full = gather_row(d_mid.astype(BF))

    block_out = (mid_rows + scatter_row(dot(activated, w_down), BF)).astype(BF)

    cot_slices = spread_left(cot_full, "z", z, shift_z)
    act_all = [activated] + [shift_z(activated, step) for step in SHIFTS]
    down_sum = finish(
        sum(dot_tn(a, b) for a, b in zip(cot_slices, act_all)), y, shift_y, xh
    ).T

    gated_all = [gated] + [shift_y(gated, step) for step in SHIFTS]
    d_up_all = [d_up] + [shift_y(d_up, step) for step in SHIFTS]
    hidden2_slices = spread_left(hidden2, "y", y, shift_y)
    up_sum = finish(
        sum(dot_tn(a, b) for a, b in zip(hidden2_slices, d_up_all)), z, shift_z, xh
    )
    d_mid_slices = spread_left(d_mid_full, "y", y, shift_y)
    output_sum = finish(
        sum(dot_tn(a, b) for a, b in zip(d_mid_slices, gated_all)), z, shift_z, xh
    ).T

    d_gated = dot_nt(d_mid_full, w_output)
    d_query, d_key, d_value, d_gate = [], [], [], []
    for h in range(2):
        decay, query, key, value, scores, group, group_factor, gate, sigmoid, silu = heads[h]
        grad = d_gated[:, h * DV : (h + 1) * DV]
        d_gate.append((grad * group * (sigmoid + silu * (1.0 - sigmoid))).astype(BF))
        d_mixed = norm_back(grad * silu, group, group_factor).astype(BF)
        d_raw = (dot_nt(d_mixed, value) * decay).astype(BF)
        d_query.append(rotate(dot(d_raw, key), cosine, -sine).astype(BF))
        d_key.append(rotate(dot_tn(d_raw, query), cosine, -sine).astype(BF))
        d_value.append(dot_tn(scores, d_mixed).astype(BF))
    d_query, d_key, d_value, d_gate = (
        jnp.concatenate(parts, axis=1) for parts in (d_query, d_key, d_value, d_gate)
    )
    total = (
        dot_nt(d_query, w_query)
        + dot_nt(d_key, w_key)
        + dot_nt(d_value, w_value)
        + dot_nt(d_gate, w_gate)
    )
    d_hidden1 = scatter_row(total, BF)
    gain1_part = jnp.sum(d_hidden1 * normed1, axis=0)
    shift1_part = jnp.sum(d_hidden1, axis=0)
    tokens_grad = d_mid + norm_back(d_hidden1 * norm1_gain, normed1, factor1)

    sums = []
    for grads in ((d_gate,), (d_value,), (d_query, d_key)):
        def columns(index):
            return jnp.concatenate([piece(g, index, g.shape[1] // 4, 1) for g in grads], axis=1)

        rights = [columns(y)] + [shift_y(columns((y + step) % 4), step) for step in SHIFTS]
        part = sum(dot_tn(a, b) for a, b in zip(hidden1_all, rights))
        part = part.reshape(4, 4, 128, 256)
        low = part.astype(BF)
        mine = lax.dynamic_index_in_dim(part, z, 1, keepdims=False)
        for step in SHIFTS:
            sent = lax.dynamic_index_in_dim(low, (z + step) % 4, 1, keepdims=False)
            mine = mine + shift_z(sent, step).astype(F32)
        mine = mine.reshape(4, 2, 64, 256)
        other = lax.dynamic_index_in_dim(mine, 1 - xh, 1, keepdims=False).astype(BF)
        mine = lax.dynamic_index_in_dim(mine, xh, 1, keepdims=False) + swap_xh(other).astype(F32)
        ready = mine.astype(BF)
        result = jnp.zeros((4, 64, 256), F32)
        result = lax.dynamic_update_index_in_dim(
            result, lax.dynamic_index_in_dim(mine, y, 0, keepdims=False), y, 0
        )
        for step in SHIFTS:
            sent = lax.dynamic_index_in_dim(ready, (y + step) % 4, 0, keepdims=False)
            got = shift_y(sent, step).astype(F32)
            result = lax.dynamic_update_index_in_dim(result, got, (y - step) % 4, 0)
        start = 0
        for g in grads:
            width = g.shape[1] // 4
            part = result[:, :, start : start + width]
            sums.append(jnp.transpose(part, (1, 0, 2)).reshape(64, 4 * width))
            start += width
    gate_sum, value_sum, query_sum, key_sum = sums

    stacked = jnp.stack([gain1_part, shift1_part, gain2_part, shift2_part], axis=0)
    spread = stacked.reshape(4, 128, 16).transpose(1, 0, 2).reshape(128, 64)
    spread = lax.all_to_all(spread, ("dp", "tensor"), 0, 0, tiled=True)
    norm_sums = jnp.sum(spread, axis=0).reshape(4, 16)
    return (
        block_out,
        tokens_grad,
        norm_sums[0],
        norm_sums[1],
        query_sum,
        key_sum,
        value_sum,
        gate_sum,
        output_sum,
        norm_sums[2],
        norm_sums[3],
        up_sum,
        down_sum,
    )


def solution(mesh):
    in_specs = (
        P(("dp", "tensor"), None),
        P("dp"),
        P(),
        P(),
        P(None, "tensor"),
        P(None, "tensor"),
        P(None, "tensor"),
        P(None, "tensor"),
        P("tensor", None),
        P(),
        P(),
        P(None, "tensor"),
        P("tensor", None),
        P(("dp", "tensor"), None),
    )
    out_specs = (
        P(("dp", "tensor"), None),
        P(("dp", "tensor"), None),
        P(("dp", "tensor")),
        P(("dp", "tensor")),
        P("dp", "tensor"),
        P("dp", "tensor"),
        P("dp", "tensor"),
        P("dp", "tensor"),
        P("tensor", "dp"),
        P(("dp", "tensor")),
        P(("dp", "tensor")),
        P("dp", "tensor"),
        P("tensor", "dp"),
    )
    return jax.shard_map(local, mesh=mesh, in_specs=in_specs, out_specs=out_specs, check_vma=False)
```

time: 2410 us -> 485 us (0.20)
  waiting for transfers between devices: 2180 us -> 182 us
  starting transfers between devices: 1.32 us -> 139 us
    reduce_scatter x11 -> x0, waiting for transfers between devices: 1440 us -> none  [the longest x1 194 us: local(): lax.psum_scatter(up_grad.astype(jnp.bfloat16), 'dp', scatter_dimension=0,...]
    unnamed x17 -> x0, waiting for transfers between devices: 631 us -> none
    ppermute x0 -> x99, waiting for transfers between devices: none -> 175 us  [the longest x36 89.7 us: shift_y(): lax.ppermute(value, 'dp', [(i, (i // 8 + step) % 4 * 8 + i % 8) for i in...]
    ppermute x0 -> x99, starting transfers between devices: none -> 130 us  [the longest x36 69.1 us: shift_y(): lax.ppermute(value, 'dp', [(i, (i // 8 + step) % 4 * 8 + i % 8) for i in...]
    all_gather x4 -> x0, waiting for transfers between devices: 112 us -> none  [the longest x1 30 us: local(): d_mid_full = lax.all_gather(d_mid_low, 'tensor', axis=0, tiled=True)]
    dot_general x27 -> x50, matrix products: 108 us -> 85.9 us  [the longest x28 40.2 us: dot_tn(): lax.dot_general(left, right, (((0,), (0,)), ((), ())), preferred_element_...]
  transfers between devices with their start and end apart: 16 -> 100, of which waited for: 16 -> 31; matrix products, arithmetic and copies ran while one was open for 3% -> 29% of each run, Pallas kernels for 0% -> 0%
where the time goes in v1:
time: 485 us; the launch traced here: 481 us
  waiting for transfers between devices  182 us (38%)
  starting transfers between devices  139 us (29%)
  matrix products  85.9 us (18%)
  other arithmetic  36.7 us (8%)
  local copies, waits for them, and re-layouts  34.8 us (7%)
    ppermute x36, waiting for transfers between devices, shift_y(): lax.ppermute(value, 'dp', [(i, (i // 8 + step) % 4 * 8 + i % 8) for i in...  89.7 us
    ppermute x36, starting transfers between devices, shift_y(): lax.ppermute(value, 'dp', [(i, (i // 8 + step) % 4 * 8 + i % 8) for i in...  69.1 us
    dot_general x28, matrix products, dot_tn(): lax.dot_general(left, right, (((0,), (0,)), ((), ())), preferred_element_...  40.2 us
    ppermute x21, waiting for transfers between devices, shift_z(): lax.ppermute(value, 'dp', [(i, i // 8 * 8 + (i // 2 % 4 + step) % 4 * 2 +...  38.8 us
    ppermute x8, waiting for transfers between devices, swap_xl(): return lax.ppermute(value, 'tensor', [(i, i ^ 2) for i in range(4)])  30.8 us
    ppermute x21, starting transfers between devices, shift_z(): lax.ppermute(value, 'dp', [(i, i // 8 * 8 + (i // 2 % 4 + step) % 4 * 2 +...  29 us
    dot_general x11, matrix products, dot(): return jnp.dot(left, right, preferred_element_type=F32)  25.2 us
    dot_general x11, matrix products, dot_nt(): lax.dot_general(left, right, (((1,), (1,)), ((), ())), preferred_element_...  20.5 us
  transfers between devices with their start and end apart: 100, of which 31 were waited for; matrix products, arithmetic and copies ran while one was open for 29% of the time, Pallas kernels for 0%

profile of v1, /device:TPU:0, one launch (start us, length us, event | category | flops | bytes accessed | tf_op | source)
XLA Modules:
  0.0 480.7 jit_solution(11642113313110039787)
XLA Ops:
  8.6 11.3 %collective-permute-done = bf16[128,2048]{1,0:T(8,128)(2,1)} collective-permute-done((bf16[128,2048]{1,0:T(8,128)(2,1)S(1)}, bf16[128,2048]{1,0:T(8,128)(2,1)}, u32[]{:S(2)}, u32[]{:S(2)}) %collective-permute-start) | collective-permute-done | bytes 524320 | tf_op jit(solution)/shard_map/ppermute | solution.py:33
  22.3 2.7 fusion.225
  25.0 2.5 fusion.226
  31.9 3.7 convolution_convert_fusion
  44.0 5.2 %fusion.227 = f32[512,1024]{1,0:T(8,128)S(1)} fusion(bf16[2048,1024]{1,0:T(8,128)(2,1)} %param.21, bf16[128,2048]{1,0:T(8,128)(2,1)} %copy-done.30, bf16[128,2048]{1,0:T(8,128)(2,1)} %collective-permute-done.1, bf16[128,2048]{1,0:T(8,128)(2,1)} %collective-permute-done, bf16[128,2048]{1,0:T(8,128)(2,1)} %copy-done.11), kind=kOutput, calls=%fused_computation.431 | convolution fusion | flops 2155872256 | bytes 8388608 | tf_op jit(solution)/shard_map/dot_general | solution.py:53
  52.5 2.3 fusion.246
  70.6 13.1 %collective-permute-done.24 = bf16[256,2048]{1,0:T(8,128)(2,1)S(1)} collective-permute-done((bf16[256,2048]{1,0:T(8,128)(2,1)S(1)}, bf16[256,2048]{1,0:T(8,128)(2,1)S(1)}, u32[]{:S(2)}, u32[]{:S(2)}) %collective-permute-start.24) | collective-permute-done | bytes 1048608 | tf_op jit(solution)/shard_map/ppermute | solution.py:15
  83.7 21.8 %collective-permute-done.27 = bf16[256,2048]{1,0:T(8,128)(2,1)S(1)} collective-permute-done((bf16[256,2048]{1,0:T(8,128)(2,1)S(1)}, bf16[256,2048]{1,0:T(8,128)(2,1)S(1)}, u32[]{:S(2)}, u32[]{:S(2)}) %collective-permute-start.27) | collective-permute-done | bytes 1048608 | tf_op jit(solution)/shard_map/ppermute | solution.py:15
  110.6 10.3 %collective-permute-done.6 = bf16[128,2048]{1,0:T(8,128)(2,1)S(1)} collective-permute-done((bf16[128,2048]{1,0:T(8,128)(2,1)S(1)}, bf16[128,2048]{1,0:T(8,128)(2,1)S(1)}, u32[]{:S(2)}, u32[]{:S(2)}) %collective-permute-start.6) | collective-permute-done | bytes 524320 | tf_op jit(solution)/shard_map/ppermute | solution.py:33
  121.6 4.0 collective-permute-start.92
  128.4 2.7 multiply_convert_fusion
  132.6 2.4 fusion.248
  135.3 4.8 fusion.12
  140.1 2.4 fusion.247
  146.2 2.4 collective-permute-start.75
  150.0 6.8 %collective-permute-done.73 = bf16[256,512]{1,0:T(8,128)(2,1)S(1)} collective-permute-done((bf16[256,512]{1,0:T(8,128)(2,1)S(1)}, bf16[256,512]{1,0:T(8,128)(2,1)S(1)}, u32[]{:S(2)}, u32[]{:S(2)}) %collective-permute-start.73) | collective-permute-done | bytes 262176 | tf_op jit(solution)/shard_map/ppermute | solution.py:15
  158.8 20.6 %collective-permute-done.88 = bf16[512,1024]{1,0:T(8,128)(2,1)S(1)} collective-permute-done((bf16[512,1024]{1,0:T(8,128)(2,1)S(1)}, bf16[512,1024]{1,0:T(8,128)(2,1)S(1)}, u32[]{:S(2)}, u32[]{:S(2)}) %collective-permute-start.88) | collective-permute-done | bytes 1048608 | tf_op jit(solution)/shard_map/ppermute | solution.py:21
  179.4 2.6 collective-permute-start.81
  187.1 20.9 %collective-permute-done.79 = bf16[256,512]{1,0:T(8,128)(2,1)S(1)} collective-permute-done((bf16[256,512]{1,0:T(8,128)(2,1)S(1)}, bf16[256,512]{1,0:T(8,128)(2,1)S(1)}, u32[]{:S(2)}, u32[]{:S(2)}) %collective-permute-start.79) | collective-permute-done | bytes 262176 | tf_op jit(solution)/shard_map/ppermute | solution.py:15
  208.3 8.9 %collective-permute-start.62 = (bf16[512,1024]{1,0:T(8,128)(2,1)}, bf16[512,1024]{1,0:T(8,128)(2,1)}, u32[]{:S(2)}, u32[]{:S(2)}) collective-permute-start(bf16[512,1024]{1,0:T(8,128)(2,1)} %pad_maximum_fusion.8), channel_id=1, source_target_pairs={{0,32},{4,36},{8,40},{12,44},{16,48},{20,52},{24,56},{28,60},{32,6... | collective-permute-start | bytes 3145736 | tf_op jit(solution)/shard_map/ppermute | solution.py:15
  222.1 2.3 fusion.252
  225.3 2.3 fusion.251
  227.5 8.6 %collective-permute-start.95 = (bf16[128,1024]{1,0:T(8,128)(2,1)}, bf16[128,1024]{1,0:T(8,128)(2,1)}, u32[]{:S(2)}, u32[]{:S(2)}) collective-permute-start(bf16[128,1024]{1,0:T(8,128)(2,1)} %get-tuple-element.63), channel_id=1, source_target_pairs={{0,32},{4,36},{8,40},{12,44},{16,48},{20,52},{24,56},{28,60},{32,6... | collective-permute-start | bytes 786440 | tf_op jit(solution)/shard_map/ppermute | solution.py:15
  236.2 9.1 %collective-permute-done.17 = bf16[128,2048]{1,0:T(8,128)(2,1)S(1)} collective-permute-done((bf16[128,2048]{1,0:T(8,128)(2,1)S(1)}, bf16[128,2048]{1,0:T(8,128)(2,1)S(1)}, u32[]{:S(2)}, u32[]{:S(2)}) %collective-permute-start.17) | collective-permute-done | bytes 524320 | tf_op jit(solution)/shard_map/ppermute | solution.py:33
  247.4 2.5 collective-permute-start.97
  257.7 3.2 collective-permute-start.83
  264.0 2.4 collective-permute-start.65
  266.4 4.9 %collective-permute-done.83 = bf16[128,1024]{1,0:T(8,128)(2,1)S(1)} collective-permute-done((bf16[128,1024]{1,0:T(8,128)(2,1)}, bf16[128,1024]{1,0:T(8,128)(2,1)S(1)}, u32[]{:S(2)}, u32[]{:S(2)}) %collective-permute-start.83) | collective-permute-done | bytes 262176 | tf_op jit(solution)/shard_map/ppermute | solution.py:21
  271.3 3.1 collective-permute-start.98
  275.9 2.9 collective-permute-done.98
  278.7 3.0 collective-permute-start.85
  282.5 2.8 collective-permute-done.85
  292.0 2.4 fusion.223
  306.3 2.4 fusion.41
  308.7 2.4 fusion.40
  317.4 6.0 %collective-permute-done.66 = bf16[256,512]{1,0:T(8,128)(2,1)S(1)} collective-permute-done((bf16[256,512]{1,0:T(8,128)(2,1)S(1)}, bf16[256,512]{1,0:T(8,128)(2,1)S(1)}, u32[]{:S(2)}, u32[]{:S(2)}) %collective-permute-start.66) | collective-permute-done | bytes 262176 | tf_op jit(solution)/shard_map/ppermute | solution.py:15
  326.0 2.8 collective-permute-start.51
  340.4 9.1 %collective-permute-done.40 = bf16[512,256]{0,1:T(8,128)(2,1)S(1)} collective-permute-done((bf16[512,256]{0,1:T(8,128)(2,1)S(1)}, bf16[512,256]{0,1:T(8,128)(2,1)S(1)}, u32[]{:S(2)}, u32[]{:S(2)}) %collective-permute-start.40) | collective-permute-done | bytes 262176 | tf_op jit(solution)/shard_map/ppermute | solution.py:15
  350.2 3.3 collective-permute-start.29
  353.5 2.3 fusion.260
  356.0 2.4 fusion.257
  358.4 2.3 fusion.261
  360.9 2.3 fusion.258
  363.2 3.7 collective-permute-start.70
  369.7 2.4 fusion.254
  372.0 2.2 fusion.5
  375.8 2.4 fusion.255
  378.2 2.2 fusion.4
  385.6 3.1 collective-permute-start.72
  388.8 3.4 collective-permute-done.72
  393.0 3.1 collective-permute-start.44
  398.9 2.9 collective-permute-done.43
  402.6 3.6 collective-permute-done.44
  409.4 3.9 collective-permute-done.33
  413.3 3.0 collective-permute-start.56
  418.1 3.0 collective-permute-start.46
  421.8 3.1 collective-permute-done.56
  429.6 4.3 collective-permute-done.37
  435.2 2.8 collective-permute-done.38
  445.7 3.0 collective-permute-start.39
  457.8 2.7 fusion.29
  461.6 8.9 %all-to-all-start = ((f32[128,1,64]{2,1,0:T(1,128)}), f32[128,1,64]{2,1,0:T(1,128)S(1)}, u32[]{:S(2)}, u32[]{:S(2)}) async-start(f32[128,1,64]{2,1,0:T(1,128)} %copy.75), calls=%async_computation | async-start | bytes 131072 | tf_op jit(solution)/shard_map/all_to_all | solution.py:280
  470.5 3.0 fusion.28
  473.4 6.3 %all-to-all-done = f32[128,1,64]{2,1,0:T(1,128)S(1)} async-done(((f32[128,1,64]{2,1,0:T(1,128)}), f32[128,1,64]{2,1,0:T(1,128)S(1)}, u32[]{:S(2)}, u32[]{:S(2)}) %all-to-all-start) | async-done | bytes 32800 | tf_op jit(solution)/shard_map/all_to_all | solution.py:280
  (470 shorter events, 168.4 us)
Async XLA Ops:
  4.9 15.0 %collective-permute-start = (bf16[128,2048]{1,0:T(8,128)(2,1)S(1)}, bf16[128,2048]{1,0:T(8,128)(2,1)}, u32[]{:S(2)}, u32[]{:S(2)}) collective-permute-start(bf16[128,2048]{1,0:T(8,128)(2,1)S(1)} %fusion.24), channel_id=1, source_target_pairs={{0,2},{1,3},{2,0},{3,1},{4,6},{5,7},{6,4},{7,5},{8,10},{9,11},{10,... | collective-permute-start | bytes 1572872 | tf_op jit(solution)/shard_map/ppermute | solution.py:33
  6.5 13.9 %collective-permute-start.1 = (bf16[128,2048]{1,0:T(8,128)(2,1)S(1)}, bf16[128,2048]{1,0:T(8,128)(2,1)}, u32[]{:S(2)}, u32[]{:S(2)}) collective-permute-start(bf16[128,2048]{1,0:T(8,128)(2,1)S(1)} %fusion.24), channel_id=1, source_target_pairs={{0,1},{1,0},{2,3},{3,2},{4,5},{5,4},{6,7},{7,6},{8,9},{9,8},{10,11... | collective-permute-start | bytes 1572872 | tf_op jit(solution)/shard_map/ppermute | solution.py:37
  7.5 52.8 %collective-permute-start.12 = (bf16[128,2048]{0,1:T(8,128)(2,1)}, bf16[128,2048]{0,1:T(8,128)(2,1)}, u32[]{:S(2)}, u32[]{:S(2)}) collective-permute-start(bf16[128,2048]{0,1:T(8,128)(2,1)} %copy.70), channel_id=1, source_target_pairs={{0,2},{1,3},{2,0},{3,1},{4,6},{5,7},{6,4},{7,5},{8,10},{9,11},{10,... | collective-permute-start | bytes 1572872 | tf_op jit(solution)/shard_map/ppermute | solution.py:33
  8.0 56.0 %collective-permute-start.13 = (bf16[128,2048]{0,1:T(8,128)(2,1)}, bf16[128,2048]{0,1:T(8,128)(2,1)}, u32[]{:S(2)}, u32[]{:S(2)}) collective-permute-start(bf16[128,2048]{0,1:T(8,128)(2,1)} %copy.70), channel_id=1, source_target_pairs={{0,1},{1,0},{2,3},{3,2},{4,5},{5,4},{6,7},{7,6},{8,9},{9,8},{10,11... | collective-permute-start | bytes 1572872 | tf_op jit(solution)/shard_map/ppermute | solution.py:37
  57.0 26.6 %collective-permute-start.24 = (bf16[256,2048]{1,0:T(8,128)(2,1)S(1)}, bf16[256,2048]{1,0:T(8,128)(2,1)S(1)}, u32[]{:S(2)}, u32[]{:S(2)}) collective-permute-start(bf16[256,2048]{1,0:T(8,128)(2,1)S(1)} %pad_maximum_fusion.9), channel_id=1, source_target_pairs={{0,32},{4,36},{8,40},{12,44},{16,48},{20,52},{24,56},{28,60},{32,6... | collective-permute-start | bytes 3145736 | tf_op jit(solution)/shard_map/ppermute | solution.py:15
  58.8 46.8 %collective-permute-start.27 = (bf16[256,2048]{1,0:T(8,128)(2,1)S(1)}, bf16[256,2048]{1,0:T(8,128)(2,1)S(1)}, u32[]{:S(2)}, u32[]{:S(2)}) collective-permute-start(bf16[256,2048]{1,0:T(8,128)(2,1)S(1)} %pad_maximum_fusion.9), channel_id=1, source_target_pairs={{0,96},{4,100},{8,104},{12,108},{16,112},{20,116},{24,120},{28,124... | collective-permute-start | bytes 3145736 | tf_op jit(solution)/shard_map/ppermute | solution.py:15
  61.8 46.4 %collective-permute-start.30 = (bf16[256,2048]{1,0:T(8,128)(2,1)S(1)}, bf16[256,2048]{1,0:T(8,128)(2,1)S(1)}, u32[]{:S(2)}, u32[]{:S(2)}) collective-permute-start(bf16[256,2048]{1,0:T(8,128)(2,1)S(1)} %pad_maximum_fusion.9), channel_id=1, source_target_pairs={{0,64},{4,68},{8,72},{12,76},{16,80},{20,84},{24,88},{28,92},{32,9... | collective-permute-start | bytes 3145736 | tf_op jit(solution)/shard_map/ppermute | solution.py:15
  64.3 41.2 %collective-permute-start.5 = (bf16[128,2048]{1,0:T(8,128)(2,1)S(1)}, bf16[128,2048]{1,0:T(8,128)(2,1)S(1)}, u32[]{:S(2)}, u32[]{:S(2)}) collective-permute-start(bf16[128,2048]{1,0:T(8,128)(2,1)S(1)} %fusion.50), channel_id=1, source_target_pairs={{0,2},{1,3},{2,0},{3,1},{4,6},{5,7},{6,4},{7,5},{8,10},{9,11},{10,... | collective-permute-start | bytes 1572872 | tf_op jit(solution)/shard_map/ppermute | solution.py:33
  68.7 74.7 %collective-permute-start.86 = (bf16[256,512]{0,1:T(8,128)(2,1)S(1)}, bf16[256,512]{0,1:T(8,128)(2,1)S(1)}, u32[]{:S(2)}, u32[]{:S(2)}) collective-permute-start(bf16[256,512]{0,1:T(8,128)(2,1)S(1)} %bitcast.222), channel_id=1, source_target_pairs={{0,8},{4,12},{8,16},{12,20},{16,24},{20,28},{24,0},{28,4},{32,40},... | collective-permute-start | bytes 786440 | tf_op jit(solution)/shard_map/ppermute | solution.py:21
  83.7 37.2 %collective-permute-start.25 = (bf16[256,2048]{1,0:T(8,128)(2,1)S(1)}, bf16[256,2048]{1,0:T(8,128)(2,1)S(1)}, u32[]{:S(2)}, u32[]{:S(2)}) collective-permute-start(bf16[256,2048]{1,0:T(8,128)(2,1)S(1)} %collective-permute-done.24), channel_id=1, source_target_pairs={{0,1},{1,0},{2,3},{3,2},{4,5},{5,4},{6,7},{7,6},{8,9},{9,8},{10,11... | collective-permute-start | bytes 3145736 | tf_op jit(solution)/shard_map/ppermute | solution.py:37
  105.5 16.1 %collective-permute-start.28 = (bf16[256,2048]{1,0:T(8,128)(2,1)S(1)}, bf16[256,2048]{1,0:T(8,128)(2,1)S(1)}, u32[]{:S(2)}, u32[]{:S(2)}) collective-permute-start(bf16[256,2048]{1,0:T(8,128)(2,1)S(1)} %collective-permute-done.27), channel_id=1, source_target_pairs={{0,1},{1,0},{2,3},{3,2},{4,5},{5,4},{6,7},{7,6},{8,9},{9,8},{10,11... | collective-permute-start | bytes 3145736 | tf_op jit(solution)/shard_map/ppermute | solution.py:37
  106.5 14.4 %collective-permute-start.6 = (bf16[128,2048]{1,0:T(8,128)(2,1)S(1)}, bf16[128,2048]{1,0:T(8,128)(2,1)S(1)}, u32[]{:S(2)}, u32[]{:S(2)}) collective-permute-start(bf16[128,2048]{1,0:T(8,128)(2,1)S(1)} %add_convert_fusion), channel_id=1, source_target_pairs={{0,2},{1,3},{2,0},{3,1},{4,6},{5,7},{6,4},{7,5},{8,10},{9,11},{10,... | collective-permute-start | bytes 1572872 | tf_op jit(solution)/shard_map/ppermute | solution.py:33
  108.2 18.4 %collective-permute-start.31 = (bf16[256,2048]{1,0:T(8,128)(2,1)S(1)}, bf16[256,2048]{1,0:T(8,128)(2,1)S(1)}, u32[]{:S(2)}, u32[]{:S(2)}) collective-permute-start(bf16[256,2048]{1,0:T(8,128)(2,1)S(1)} %collective-permute-done.30), channel_id=1, source_target_pairs={{0,1},{1,0},{2,3},{3,2},{4,5},{5,4},{6,7},{7,6},{8,9},{9,8},{10,11... | collective-permute-start | bytes 3145736 | tf_op jit(solution)/shard_map/ppermute | solution.py:37
  121.6 22.5 %collective-permute-start.92 = (bf16[256,512]{0,1:T(8,128)(2,1)S(1)}, bf16[256,512]{0,1:T(8,128)(2,1)S(1)}, u32[]{:S(2)}, u32[]{:S(2)}) collective-permute-start(bf16[256,512]{0,1:T(8,128)(2,1)S(1)} %bitcast.221), channel_id=1, source_target_pairs={{0,16},{4,20},{8,24},{12,28},{16,0},{20,4},{24,8},{28,12},{32,48},... | collective-permute-start | bytes 786440 | tf_op jit(solution)/shard_map/ppermute | solution.py:21
  126.6 17.6 %collective-permute-start.89 = (bf16[256,512]{0,1:T(8,128)(2,1)S(1)}, bf16[256,512]{0,1:T(8,128)(2,1)S(1)}, u32[]{:S(2)}, u32[]{:S(2)}) collective-permute-start(bf16[256,512]{0,1:T(8,128)(2,1)S(1)} %bitcast.220), channel_id=1, source_target_pairs={{0,24},{4,28},{8,0},{12,4},{16,8},{20,12},{24,16},{28,20},{32,56},... | collective-permute-start | bytes 786440 | tf_op jit(solution)/shard_map/ppermute | solution.py:21
  131.2 48.3 %collective-permute-start.88 = (bf16[512,1024]{1,0:T(8,128)(2,1)S(1)}, bf16[512,1024]{1,0:T(8,128)(2,1)S(1)}, u32[]{:S(2)}, u32[]{:S(2)}) collective-permute-start(bf16[512,1024]{1,0:T(8,128)(2,1)S(1)} %get-tuple-element.152), channel_id=1, source_target_pairs={{0,8},{4,12},{8,16},{12,20},{16,24},{20,28},{24,0},{28,4},{32,40},... | collective-permute-start | bytes 3145736 | tf_op jit(solution)/shard_map/ppermute | solution.py:21
  144.8 38.1 %collective-permute-start.94 = (bf16[512,1024]{1,0:T(8,128)(2,1)S(1)}, bf16[512,1024]{1,0:T(8,128)(2,1)S(1)}, u32[]{:S(2)}, u32[]{:S(2)}) collective-permute-start(bf16[512,1024]{1,0:T(8,128)(2,1)S(1)} %get-tuple-element.152), channel_id=1, source_target_pairs={{0,16},{4,20},{8,24},{12,28},{16,0},{20,4},{24,8},{28,12},{32,48},... | collective-permute-start | bytes 3145736 | tf_op jit(solution)/shard_map/ppermute | solution.py:21
  146.2 40.2 %collective-permute-start.75 = (bf16[512,1024]{1,0:T(8,128)(2,1)S(1)}, bf16[512,1024]{1,0:T(8,128)(2,1)S(1)}, u32[]{:S(2)}, u32[]{:S(2)}) collective-permute-start(bf16[512,1024]{1,0:T(8,128)(2,1)S(1)} %fusion.12), channel_id=1, source_target_pairs={{0,32},{4,36},{8,40},{12,44},{16,48},{20,52},{24,56},{28,60},{32,6... | collective-permute-start | bytes 3145736 | tf_op jit(solution)/shard_map/ppermute | solution.py:15
  148.6 68.6 %collective-permute-start.78 = (bf16[512,1024]{1,0:T(8,128)(2,1)S(1)}, bf16[512,1024]{1,0:T(8,128)(2,1)S(1)}, u32[]{:S(2)}, u32[]{:S(2)}) collective-permute-start(bf16[512,1024]{1,0:T(8,128)(2,1)S(1)} %fusion.12), channel_id=1, source_target_pairs={{0,96},{4,100},{8,104},{12,108},{16,112},{20,116},{24,120},{28,124... | collective-permute-start | bytes 3145736 | tf_op jit(solution)/shard_map/ppermute | solution.py:15
  156.8 26.0 %collective-permute-start.76 = (bf16[256,512]{1,0:T(8,128)(2,1)S(1)}, bf16[256,512]{1,0:T(8,128)(2,1)S(1)}, u32[]{:S(2)}, u32[]{:S(2)}) collective-permute-start(bf16[256,512]{1,0:T(8,128)(2,1)S(1)} %get-tuple-element.73), channel_id=1, source_target_pairs={{0,96},{4,100},{8,104},{12,108},{16,112},{20,116},{24,120},{28,124... | collective-permute-start | bytes 786440 | tf_op jit(solution)/shard_map/ppermute | solution.py:15
  179.4 39.4 %collective-permute-start.81 = (bf16[512,1024]{1,0:T(8,128)(2,1)S(1)}, bf16[512,1024]{1,0:T(8,128)(2,1)S(1)}, u32[]{:S(2)}, u32[]{:S(2)}) collective-permute-start(bf16[512,1024]{1,0:T(8,128)(2,1)S(1)} %fusion.12), channel_id=1, source_target_pairs={{0,64},{4,68},{8,72},{12,76},{16,80},{20,84},{24,88},{28,92},{32,9... | collective-permute-start | bytes 3145736 | tf_op jit(solution)/shard_map/ppermute | solution.py:15
  182.8 38.7 %collective-permute-start.91 = (bf16[512,1024]{1,0:T(8,128)(2,1)S(1)}, bf16[512,1024]{1,0:T(8,128)(2,1)S(1)}, u32[]{:S(2)}, u32[]{:S(2)}) collective-permute-start(bf16[512,1024]{1,0:T(8,128)(2,1)S(1)} %get-tuple-element.152), channel_id=1, source_target_pairs={{0,24},{4,28},{8,0},{12,4},{16,8},{20,12},{24,16},{28,20},{32,56},... | collective-permute-start | bytes 3145736 | tf_op jit(solution)/shard_map/ppermute | solution.py:21
  184.3 23.7 %collective-permute-start.79 = (bf16[256,512]{1,0:T(8,128)(2,1)S(1)}, bf16[256,512]{1,0:T(8,128)(2,1)S(1)}, u32[]{:S(2)}, u32[]{:S(2)}) collective-permute-start(bf16[256,512]{1,0:T(8,128)(2,1)S(1)} %get-tuple-element.74), channel_id=1, source_target_pairs={{0,64},{4,68},{8,72},{12,76},{16,80},{20,84},{24,88},{28,92},{32,9... | collective-permute-start | bytes 786440 | tf_op jit(solution)/shard_map/ppermute | solution.py:15
  186.4 21.9 %collective-permute-start.77 = (bf16[256,512]{1,0:T(8,128)(2,1)S(1)}, bf16[256,512]{1,0:T(8,128)(2,1)S(1)}, u32[]{:S(2)}, u32[]{:S(2)}) collective-permute-start(bf16[256,512]{1,0:T(8,128)(2,1)S(1)} %collective-permute-done.76), channel_id=1, source_target_pairs={{0,1},{1,0},{2,3},{3,2},{4,5},{5,4},{6,7},{7,6},{8,9},{9,8},{10,11... | collective-permute-start | bytes 786440 | tf_op jit(solution)/shard_map/ppermute | solution.py:37
  208.3 107.2 %collective-permute-start.62 = (bf16[512,1024]{1,0:T(8,128)(2,1)}, bf16[512,1024]{1,0:T(8,128)(2,1)}, u32[]{:S(2)}, u32[]{:S(2)}) collective-permute-start(bf16[512,1024]{1,0:T(8,128)(2,1)} %pad_maximum_fusion.8), channel_id=1, source_target_pairs={{0,32},{4,36},{8,40},{12,44},{16,48},{20,52},{24,56},{28,60},{32,6... | collective-permute-start | bytes 3145736 | tf_op jit(solution)/shard_map/ppermute | solution.py:15
  218.9 28.5 %collective-permute-start.9 = (bf16[128,2048]{1,0:T(8,128)(2,1)S(1)}, bf16[128,2048]{1,0:T(8,128)(2,1)S(1)}, u32[]{:S(2)}, u32[]{:S(2)}) collective-permute-start(bf16[128,2048]{1,0:T(8,128)(2,1)S(1)} %get-tuple-element.49), channel_id=1, source_target_pairs={{0,1},{1,0},{2,3},{3,2},{4,5},{5,4},{6,7},{7,6},{8,9},{9,8},{10,11... | collective-permute-start | bytes 1572872 | tf_op jit(solution)/shard_map/ppermute | solution.py:37
  220.0 29.9 %collective-permute-start.11 = (bf16[128,2048]{1,0:T(8,128)(2,1)S(1)}, bf16[128,2048]{1,0:T(8,128)(2,1)S(1)}, u32[]{:S(2)}, u32[]{:S(2)}) collective-permute-start(bf16[128,2048]{1,0:T(8,128)(2,1)S(1)} %fusion.46), channel_id=1, source_target_pairs={{0,2},{1,3},{2,0},{3,1},{4,6},{5,7},{6,4},{7,5},{8,10},{9,11},{10,... | collective-permute-start | bytes 1572872 | tf_op jit(solution)/shard_map/ppermute | solution.py:33
  221.6 23.7 %collective-permute-start.17 = (bf16[128,2048]{1,0:T(8,128)(2,1)S(1)}, bf16[128,2048]{1,0:T(8,128)(2,1)S(1)}, u32[]{:S(2)}, u32[]{:S(2)}) collective-permute-start(bf16[128,2048]{1,0:T(8,128)(2,1)S(1)} %fusion.44), channel_id=1, source_target_pairs={{0,2},{1,3},{2,0},{3,1},{4,6},{5,7},{6,4},{7,5},{8,10},{9,11},{10,... | collective-permute-start | bytes 1572872 | tf_op jit(solution)/shard_map/ppermute | solution.py:33
  227.5 30.2 %collective-permute-start.95 = (bf16[128,1024]{1,0:T(8,128)(2,1)}, bf16[128,1024]{1,0:T(8,128)(2,1)}, u32[]{:S(2)}, u32[]{:S(2)}) collective-permute-start(bf16[128,1024]{1,0:T(8,128)(2,1)} %get-tuple-element.63), channel_id=1, source_target_pairs={{0,32},{4,36},{8,40},{12,44},{16,48},{20,52},{24,56},{28,60},{32,6... | collective-permute-start | bytes 786440 | tf_op jit(solution)/shard_map/ppermute | solution.py:15
  245.3 15.7 %collective-permute-start.96 = (bf16[128,1024]{1,0:T(8,128)(2,1)}, bf16[128,1024]{1,0:T(8,128)(2,1)}, u32[]{:S(2)}, u32[]{:S(2)}) collective-permute-start(bf16[128,1024]{1,0:T(8,128)(2,1)} %get-tuple-element.65), channel_id=1, source_target_pairs={{0,96},{4,100},{8,104},{12,108},{16,112},{20,116},{24,120},{28,124... | collective-permute-start | bytes 786440 | tf_op jit(solution)/shard_map/ppermute | solution.py:15
  247.4 13.6 %collective-permute-start.97 = (bf16[128,1024]{1,0:T(8,128)(2,1)}, bf16[128,1024]{1,0:T(8,128)(2,1)}, u32[]{:S(2)}, u32[]{:S(2)}) collective-permute-start(bf16[128,1024]{1,0:T(8,128)(2,1)} %get-tuple-element.64), channel_id=1, source_target_pairs={{0,64},{4,68},{8,72},{12,76},{16,80},{20,84},{24,88},{28,92},{32,9... | collective-permute-start | bytes 786440 | tf_op jit(solution)/shard_map/ppermute | solution.py:15
  249.9 14.2 %collective-permute-start.82 = (bf16[128,1024]{1,0:T(8,128)(2,1)}, bf16[128,1024]{1,0:T(8,128)(2,1)}, u32[]{:S(2)}, u32[]{:S(2)}) collective-permute-start(bf16[128,1024]{1,0:T(8,128)(2,1)} %get-tuple-element.69), channel_id=1, source_target_pairs={{0,8},{4,12},{8,16},{12,20},{16,24},{20,28},{24,0},{28,4},{32,40},... | collective-permute-start | bytes 786440 | tf_op jit(solution)/shard_map/ppermute | solution.py:21
  257.7 13.6 %collective-permute-start.83 = (bf16[128,1024]{1,0:T(8,128)(2,1)}, bf16[128,1024]{1,0:T(8,128)(2,1)S(1)}, u32[]{:S(2)}, u32[]{:S(2)}) collective-permute-start(bf16[128,1024]{1,0:T(8,128)(2,1)} %get-tuple-element.71), channel_id=1, source_target_pairs={{0,24},{4,28},{8,0},{12,4},{16,8},{20,12},{24,16},{28,20},{32,56},... | collective-permute-start | bytes 786440 | tf_op jit(solution)/shard_map/ppermute | solution.py:21
  261.0 20.8 %collective-permute-start.18 = (bf16[128,2048]{1,0:T(8,128)(2,1)}, bf16[128,2048]{1,0:T(8,128)(2,1)S(1)}, u32[]{:S(2)}, u32[]{:S(2)}) collective-permute-start(bf16[128,2048]{1,0:T(8,128)(2,1)} %get-tuple-element.34), channel_id=1, source_target_pairs={{0,2},{1,3},{2,0},{3,1},{4,6},{5,7},{6,4},{7,5},{8,10},{9,11},{10,... | collective-permute-start | bytes 1572872 | tf_op jit(solution)/shard_map/ppermute | solution.py:33
  264.0 62.0 %collective-permute-start.65 = (bf16[512,1024]{1,0:T(8,128)(2,1)}, bf16[512,1024]{1,0:T(8,128)(2,1)}, u32[]{:S(2)}, u32[]{:S(2)}) collective-permute-start(bf16[512,1024]{1,0:T(8,128)(2,1)} %pad_maximum_fusion.8), channel_id=1, source_target_pairs={{0,96},{4,100},{8,104},{12,108},{16,112},{20,116},{24,120},{28,124... | collective-permute-start | bytes 3145736 | tf_op jit(solution)/shard_map/ppermute | solution.py:15
  271.3 16.9 %collective-permute-start.19 = (bf16[128,2048]{1,0:T(8,128)(2,1)S(1)}, bf16[128,2048]{1,0:T(8,128)(2,1)S(1)}, u32[]{:S(2)}, u32[]{:S(2)}) collective-permute-start(bf16[128,2048]{1,0:T(8,128)(2,1)S(1)} %copy-done.18), channel_id=1, source_target_pairs={{0,1},{1,0},{2,3},{3,2},{4,5},{5,4},{6,7},{7,6},{8,9},{9,8},{10,11... | collective-permute-start | bytes 1572872 | tf_op jit(solution)/shard_map/ppermute | solution.py:37
  285.3 45.9 %collective-permute-start.68 = (bf16[512,1024]{1,0:T(8,128)(2,1)}, bf16[512,1024]{1,0:T(8,128)(2,1)}, u32[]{:S(2)}, u32[]{:S(2)}) collective-permute-start(bf16[512,1024]{1,0:T(8,128)(2,1)} %pad_maximum_fusion.8), channel_id=1, source_target_pairs={{0,64},{4,68},{8,72},{12,76},{16,80},{20,84},{24,88},{28,92},{32,9... | collective-permute-start | bytes 3145736 | tf_op jit(solution)/shard_map/ppermute | solution.py:15
  288.2 28.3 %collective-permute-start.60 = (bf16[256,512]{1,0:T(8,128)(2,1)}, bf16[256,512]{1,0:T(8,128)(2,1)}, u32[]{:S(2)}, u32[]{:S(2)}) collective-permute-start(bf16[256,512]{1,0:T(8,128)(2,1)} %get-tuple-element.78), channel_id=1, source_target_pairs={{0,32},{4,36},{8,40},{12,44},{16,48},{20,52},{24,56},{28,60},{32,6... | collective-permute-start | bytes 786440 | tf_op jit(solution)/shard_map/ppermute | solution.py:15
  290.0 26.8 %collective-permute-start.63 = (bf16[256,512]{1,0:T(8,128)(2,1)}, bf16[256,512]{1,0:T(8,128)(2,1)}, u32[]{:S(2)}, u32[]{:S(2)}) collective-permute-start(bf16[256,512]{1,0:T(8,128)(2,1)} %get-tuple-element.79), channel_id=1, source_target_pairs={{0,96},{4,100},{8,104},{12,108},{16,112},{20,116},{24,120},{28,124... | collective-permute-start | bytes 786440 | tf_op jit(solution)/shard_map/ppermute | solution.py:15
  323.4 15.2 %collective-permute-start.50 = (bf16[512,256]{1,0:T(8,128)(2,1)S(1)}, bf16[512,256]{1,0:T(8,128)(2,1)S(1)}, u32[]{:S(2)}, u32[]{:S(2)}) collective-permute-start(bf16[512,256]{1,0:T(8,128)(2,1)S(1)} %get-tuple-element.84), channel_id=1, source_target_pairs={{0,32},{4,36},{8,40},{12,44},{16,48},{20,52},{24,56},{28,60},{32,6... | collective-permute-start | bytes 786440 | tf_op jit(solution)/shard_map/ppermute | solution.py:15
  326.0 24.2 %collective-permute-start.51 = (bf16[512,256]{1,0:T(8,128)(2,1)S(1)}, bf16[512,256]{1,0:T(8,128)(2,1)S(1)}, u32[]{:S(2)}, u32[]{:S(2)}) collective-permute-start(bf16[512,256]{1,0:T(8,128)(2,1)S(1)} %get-tuple-element.85), channel_id=1, source_target_pairs={{0,96},{4,100},{8,104},{12,108},{16,112},{20,116},{24,120},{28,124... | collective-permute-start | bytes 786440 | tf_op jit(solution)/shard_map/ppermute | solution.py:15
  328.8 29.6 %collective-permute-start.52 = (bf16[512,256]{1,0:T(8,128)(2,1)S(1)}, bf16[512,256]{1,0:T(8,128)(2,1)S(1)}, u32[]{:S(2)}, u32[]{:S(2)}) collective-permute-start(bf16[512,256]{1,0:T(8,128)(2,1)S(1)} %get-tuple-element.86), channel_id=1, source_target_pairs={{0,64},{4,68},{8,72},{12,76},{16,80},{20,84},{24,88},{28,92},{32,9... | collective-permute-start | bytes 786440 | tf_op jit(solution)/shard_map/ppermute | solution.py:15
  331.2 18.3 %collective-permute-start.40 = (bf16[512,256]{0,1:T(8,128)(2,1)S(1)}, bf16[512,256]{0,1:T(8,128)(2,1)S(1)}, u32[]{:S(2)}, u32[]{:S(2)}) collective-permute-start(bf16[512,256]{0,1:T(8,128)(2,1)S(1)} %get-tuple-element.90), channel_id=1, source_target_pairs={{0,32},{4,36},{8,40},{12,44},{16,48},{20,52},{24,56},{28,60},{32,6... | collective-permute-start | bytes 786440 | tf_op jit(solution)/shard_map/ppermute | solution.py:15
  332.6 23.3 %collective-permute-start.41 = (bf16[512,256]{0,1:T(8,128)(2,1)S(1)}, bf16[512,256]{0,1:T(8,128)(2,1)S(1)}, u32[]{:S(2)}, u32[]{:S(2)}) collective-permute-start(bf16[512,256]{0,1:T(8,128)(2,1)S(1)} %get-tuple-element.91), channel_id=1, source_target_pairs={{0,96},{4,100},{8,104},{12,108},{16,112},{20,116},{24,120},{28,124... | collective-permute-start | bytes 786440 | tf_op jit(solution)/shard_map/ppermute | solution.py:15
  338.6 22.2 %collective-permute-start.42 = (bf16[512,256]{0,1:T(8,128)(2,1)S(1)}, bf16[512,256]{0,1:T(8,128)(2,1)S(1)}, u32[]{:S(2)}, u32[]{:S(2)}) collective-permute-start(bf16[512,256]{0,1:T(8,128)(2,1)S(1)} %get-tuple-element.92), channel_id=1, source_target_pairs={{0,64},{4,68},{8,72},{12,76},{16,80},{20,84},{24,88},{28,92},{32,9... | collective-permute-start | bytes 786440 | tf_op jit(solution)/shard_map/ppermute | solution.py:15
  349.4 13.8 %collective-permute-start.26 = (bf16[512,256]{0,1:T(8,128)(2,1)S(1)}, bf16[512,256]{0,1:T(8,128)(2,1)S(1)}, u32[]{:S(2)}, u32[]{:S(2)}) collective-permute-start(bf16[512,256]{0,1:T(8,128)(2,1)S(1)} %pad_maximum_fusion.17), channel_id=1, source_target_pairs={{0,32},{4,36},{8,40},{12,44},{16,48},{20,52},{24,56},{28,60},{32,6... | collective-permute-start | bytes 786440 | tf_op jit(solution)/shard_map/ppermute | solution.py:15
  350.2 17.5 %collective-permute-start.29 = (bf16[512,256]{0,1:T(8,128)(2,1)S(1)}, bf16[512,256]{0,1:T(8,128)(2,1)S(1)}, u32[]{:S(2)}, u32[]{:S(2)}) collective-permute-start(bf16[512,256]{0,1:T(8,128)(2,1)S(1)} %pad_maximum_fusion.18), channel_id=1, source_target_pairs={{0,96},{4,100},{8,104},{12,108},{16,112},{20,116},{24,120},{28,124... | collective-permute-start | bytes 786440 | tf_op jit(solution)/shard_map/ppermute | solution.py:15
  355.9 18.5 %collective-permute-start.32 = (bf16[512,256]{0,1:T(8,128)(2,1)S(1)}, bf16[512,256]{0,1:T(8,128)(2,1)S(1)}, u32[]{:S(2)}, u32[]{:S(2)}) collective-permute-start(bf16[512,256]{0,1:T(8,128)(2,1)S(1)} %pad_maximum_fusion.19), channel_id=1, source_target_pairs={{0,64},{4,68},{8,72},{12,76},{16,80},{20,84},{24,88},{28,92},{32,9... | collective-permute-start | bytes 786440 | tf_op jit(solution)/shard_map/ppermute | solution.py:15
  358.3 34.6 %collective-permute-start.22 = (bf16[128,2048]{1,0:T(8,128)(2,1)S(1)}, bf16[128,2048]{1,0:T(8,128)(2,1)S(1)}, u32[]{:S(2)}, u32[]{:S(2)}) collective-permute-start(bf16[128,2048]{1,0:T(8,128)(2,1)S(1)} %get-tuple-element.46), channel_id=1, source_target_pairs={{0,1},{1,0},{2,3},{3,2},{4,5},{5,4},{6,7},{7,6},{8,9},{9,8},{10,11... | collective-permute-start | bytes 1572872 | tf_op jit(solution)/shard_map/ppermute | solution.py:37
  360.8 21.9 %collective-permute-start.69 = (bf16[128,1024]{1,0:T(8,128)(2,1)S(1)}, bf16[128,1024]{1,0:T(8,128)(2,1)S(1)}, u32[]{:S(2)}, u32[]{:S(2)}) collective-permute-start(bf16[128,1024]{1,0:T(8,128)(2,1)S(1)} %get-tuple-element.75), channel_id=1, source_target_pairs={{0,8},{4,12},{8,16},{12,20},{16,24},{20,28},{24,0},{28,4},{32,40},... | collective-permute-start | bytes 786440 | tf_op jit(solution)/shard_map/ppermute | solution.py:21
  363.2 21.3 %collective-permute-start.70 = (bf16[128,1024]{1,0:T(8,128)(2,1)S(1)}, bf16[128,1024]{1,0:T(8,128)(2,1)S(1)}, u32[]{:S(2)}, u32[]{:S(2)}) collective-permute-start(bf16[128,1024]{1,0:T(8,128)(2,1)S(1)} %get-tuple-element.77), channel_id=1, source_target_pairs={{0,24},{4,28},{8,0},{12,4},{16,8},{20,12},{24,16},{28,20},{32,56},... | collective-permute-start | bytes 786440 | tf_op jit(solution)/shard_map/ppermute | solution.py:21
  367.7 17.7 %collective-permute-start.71 = (bf16[128,1024]{1,0:T(8,128)(2,1)S(1)}, bf16[128,1024]{1,0:T(8,128)(2,1)S(1)}, u32[]{:S(2)}, u32[]{:S(2)}) collective-permute-start(bf16[128,1024]{1,0:T(8,128)(2,1)S(1)} %get-tuple-element.76), channel_id=1, source_target_pairs={{0,16},{4,20},{8,24},{12,28},{16,0},{20,4},{24,8},{28,12},{32,48},... | collective-permute-start | bytes 786440 | tf_op jit(solution)/shard_map/ppermute | solution.py:21
  374.4 21.8 %collective-permute-start.53 = (bf16[4,128,256]{2,1,0:T(8,128)(2,1)S(1)}, bf16[4,128,256]{2,1,0:T(8,128)(2,1)S(1)}, u32[]{:S(2)}, u32[]{:S(2)}) collective-permute-start(bf16[4,128,256]{2,1,0:T(8,128)(2,1)S(1)} %get-tuple-element.81), channel_id=1, source_target_pairs={{0,8},{4,12},{8,16},{12,20},{16,24},{20,28},{24,0},{28,4},{32,40},... | collective-permute-start | bytes 786440 | tf_op jit(solution)/shard_map/ppermute | solution.py:21
  382.7 15.8 %collective-permute-start.54 = (bf16[4,128,256]{2,1,0:T(8,128)(2,1)S(1)}, bf16[4,128,256]{2,1,0:T(8,128)(2,1)S(1)}, u32[]{:S(2)}, u32[]{:S(2)}) collective-permute-start(bf16[4,128,256]{2,1,0:T(8,128)(2,1)S(1)} %get-tuple-element.83), channel_id=1, source_target_pairs={{0,24},{4,28},{8,0},{12,4},{16,8},{20,12},{24,16},{28,20},{32,56},... | collective-permute-start | bytes 786440 | tf_op jit(solution)/shard_map/ppermute | solution.py:21
  384.6 13.9 %collective-permute-start.55 = (bf16[4,128,256]{2,1,0:T(8,128)(2,1)S(1)}, bf16[4,128,256]{2,1,0:T(8,128)(2,1)S(1)}, u32[]{:S(2)}, u32[]{:S(2)}) collective-permute-start(bf16[4,128,256]{2,1,0:T(8,128)(2,1)S(1)} %get-tuple-element.82), channel_id=1, source_target_pairs={{0,16},{4,20},{8,24},{12,28},{16,0},{20,4},{24,8},{28,12},{32,48},... | collective-permute-start | bytes 786440 | tf_op jit(solution)/shard_map/ppermute | solution.py:21
  393.0 13.2 %collective-permute-start.44 = (bf16[4,128,256]{2,1,0:T(8,128)(2,1)S(1)}, bf16[4,128,256]{2,1,0:T(8,128)(2,1)S(1)}, u32[]{:S(2)}, u32[]{:S(2)}) collective-permute-start(bf16[4,128,256]{2,1,0:T(8,128)(2,1)S(1)} %get-tuple-element.89), channel_id=1, source_target_pairs={{0,24},{4,28},{8,0},{12,4},{16,8},{20,12},{24,16},{28,20},{32,56},... | collective-permute-start | bytes 786440 | tf_op jit(solution)/shard_map/ppermute | solution.py:21
  398.5 59.2 %collective-permute-start.21 = (bf16[128,2048]{1,0:T(8,128)(2,1)}, bf16[128,2048]{1,0:T(8,128)(2,1)S(1)}, u32[]{:S(2)}, u32[]{:S(2)}) collective-permute-start(bf16[128,2048]{1,0:T(8,128)(2,1)} %get-tuple-element.45), channel_id=1, source_target_pairs={{0,1},{1,0},{2,3},{3,2},{4,5},{5,4},{6,7},{7,6},{8,9},{9,8},{10,11... | collective-permute-start | bytes 1572872 | tf_op jit(solution)/shard_map/ppermute | solution.py:37
  398.5 14.8 %collective-permute-start.33 = (bf16[4,128,256]{2,1,0:T(8,128)(2,1)S(1)}, bf16[4,128,256]{2,1,0:T(8,128)(2,1)S(1)}, u32[]{:S(2)}, u32[]{:S(2)}) collective-permute-start(bf16[4,128,256]{2,1,0:T(8,128)(2,1)S(1)} %get-tuple-element.93), channel_id=1, source_target_pairs={{0,8},{4,12},{8,16},{12,20},{16,24},{20,28},{24,0},{28,4},{32,40},... | collective-permute-start | bytes 786440 | tf_op jit(solution)/shard_map/ppermute | solution.py:21
  401.8 16.3 %collective-permute-start.34 = (bf16[4,128,256]{2,1,0:T(8,128)(2,1)S(1)}, bf16[4,128,256]{2,1,0:T(8,128)(2,1)S(1)}, u32[]{:S(2)}, u32[]{:S(2)}) collective-permute-start(bf16[4,128,256]{2,1,0:T(8,128)(2,1)S(1)} %get-tuple-element.95), channel_id=1, source_target_pairs={{0,24},{4,28},{8,0},{12,4},{16,8},{20,12},{24,16},{28,20},{32,56},... | collective-permute-start | bytes 786440 | tf_op jit(solution)/shard_map/ppermute | solution.py:21
  406.2 14.9 %collective-permute-start.35 = (bf16[4,128,256]{2,1,0:T(8,128)(2,1)S(1)}, bf16[4,128,256]{2,1,0:T(8,128)(2,1)S(1)}, u32[]{:S(2)}, u32[]{:S(2)}) collective-permute-start(bf16[4,128,256]{2,1,0:T(8,128)(2,1)S(1)} %get-tuple-element.94), channel_id=1, source_target_pairs={{0,16},{4,20},{8,24},{12,28},{16,0},{20,4},{24,8},{28,12},{32,48},... | collective-permute-start | bytes 786440 | tf_op jit(solution)/shard_map/ppermute | solution.py:21
  407.7 50.1 %collective-permute-start.23 = (bf16[128,2048]{1,0:T(8,128)(2,1)}, bf16[128,2048]{1,0:T(8,128)(2,1)}, u32[]{:S(2)}, u32[]{:S(2)}) collective-permute-start(bf16[128,2048]{1,0:T(8,128)(2,1)} %fusion.42), channel_id=1, source_target_pairs={{0,2},{1,3},{2,0},{3,1},{4,6},{5,7},{6,4},{7,5},{8,10},{9,11},{10,... | collective-permute-start | bytes 1572872 | tf_op jit(solution)/shard_map/ppermute | solution.py:33
  425.1 14.8 %collective-permute-start.57 = (bf16[64,256]{1,0:T(8,128)(2,1)S(1)}, bf16[64,256]{1,0:T(8,128)(2,1)S(1)}, u32[]{:S(2)}, u32[]{:S(2)}) collective-permute-start(bf16[64,256]{1,0:T(8,128)(2,1)S(1)} %get-tuple-element.117), channel_id=1, source_target_pairs={{0,32},{4,36},{8,40},{12,44},{16,48},{20,52},{24,56},{28,60},{32,6... | collective-permute-start | bytes 98312 | tf_op jit(solution)/shard_map/ppermute | solution.py:15
  426.9 14.4 %collective-permute-start.58 = (bf16[64,256]{1,0:T(8,128)(2,1)S(1)}, bf16[64,256]{1,0:T(8,128)(2,1)S(1)}, u32[]{:S(2)}, u32[]{:S(2)}) collective-permute-start(bf16[64,256]{1,0:T(8,128)(2,1)S(1)} %get-tuple-element.116), channel_id=1, source_target_pairs={{0,96},{4,100},{8,104},{12,108},{16,112},{20,116},{24,120},{28,124... | collective-permute-start | bytes 98312 | tf_op jit(solution)/shard_map/ppermute | solution.py:15
  461.6 18.2 %all-to-all-start = ((f32[128,1,64]{2,1,0:T(1,128)}), f32[128,1,64]{2,1,0:T(1,128)S(1)}, u32[]{:S(2)}, u32[]{:S(2)}) async-start(f32[128,1,64]{2,1,0:T(1,128)} %copy.75), calls=%async_computation | async-start | bytes 131072 | tf_op jit(solution)/shard_map/all_to_all | solution.py:280
  (107 other events, 878.5 us)
